TPU v7x, 128 devices: a whole 4x4x4 slice. The times are simulated.
128 devices in a mesh: pipe: 4 (over y_lo, core), dp: 32 (over y_hi, z, x).
Axes of the slice: x: 4, y: 4 (y_hi: 2, y_lo: 2; y = y_hi * 2 + y_lo), z: 4, core: 2. Of those that a mesh axis runs over, the one named last changes fastest.
Arguments:
- stash: bfloat16 [4, 2, 5120, 6144], P('pipe', None, 'dp'), may hold values from -6 to 6
- attn: bfloat16 [4, 2, 32, 6, 160, 160], P('pipe', None, 'dp'), may hold values from 0 to 0.03930664
- w_value: bfloat16 [4, 6144, 768], P('pipe'), may hold values from -0.078125 to 0.078125
- w_out: bfloat16 [4, 768, 6144], P('pipe'), may hold values from -0.21875 to 0.21875
- out_grad: bfloat16 [2, 5120, 6144], P(None, 'dp', 'pipe'), may hold values from -6 to 6
- order: int32 [2], replicated, may hold values from 0 to 1, each once
- check_rows: int32 [8, 6144], replicated, may hold values from -3 to 3
Outputs:
- grad_value: float32 [4, 6144, 768], P('pipe', 'dp')
- grad_out_t: float32 [4, 6144, 768], P('pipe', 'dp')
- checksums: float32 [4, 2, 8, 768], P('pipe')
- input_grad: bfloat16 [2, 5120, 6144], P(None, 'dp', 'pipe')
Inputs may be any that keep to these rules, and one draw needn't show every extreme that they name: `order`: a permutation of the micro-batches.
All inputs are finite; a program needn't handle non-finite values.
Results may differ from a plain program's by a relative error of at most 0.022.
Values may be sent and summed in bfloat16 or wider, within the bound.
No kernel may reach another device: no remote copies, remote signals or barrier semaphores. Data moves between devices by JAX's collectives and lax.ppermute only.
A program may use at most 192 MiB of HBM per device.

v0:
```python
import jax
import jax.numpy as jnp
from jax import lax
from jax.sharding import PartitionSpec as P


def passed_along(block, axis, distance):
    devices = range(lax.axis_size(axis))
    route = [(i - distance, i) for i in devices if i - distance in devices]
    return lax.ppermute(block, axis, route)


def from_root(array, axis, root):
    mine = lax.axis_index(axis) == root
    return lax.psum(jnp.where(mine, array, jnp.zeros_like(array)), axis)


def on_device(stash, attn, w_value, w_out, out_grad, order, check_rows):
    npipe = lax.axis_size("pipe")
    section = lax.axis_index("pipe")
    inputs = stash[0]
    probs = attn[0][:, 0]
    wv = w_value[0]
    wo = w_out[0]
    micro = inputs.shape[0]
    seq = inputs.shape[1]
    width = inputs.shape[2]
    inner = wv.shape[1]
    heads = probs.shape[1]
    head_dim = inner // heads
    grad_scale = jnp.float32((micro * seq * lax.axis_size("dp")) ** (-0.5))
    check_scale = jnp.float32(width ** (-0.5))
    causal = (jnp.arange(seq)[:, None] >= jnp.arange(seq)[None, :]).astype(jnp.bfloat16)
    top_grad = lax.all_gather(out_grad, "pipe", axis=2, tiled=True)

    def backward_step(operands):
        xm, pm, dy = operands
        weights = pm * causal
        values = jnp.dot(xm, wv, preferred_element_type=jnp.float32).astype(jnp.bfloat16)
        context = jnp.einsum(
            "hij,jhd->ihd",
            weights,
            values.reshape(seq, heads, head_dim),
            preferred_element_type=jnp.float32,
        )
        context = context.reshape(seq, inner).astype(jnp.bfloat16)
        dctx = jnp.dot(dy, wo.T, preferred_element_type=jnp.float32).astype(jnp.bfloat16)
        dvals = jnp.einsum(
            "hij,ihd->jhd",
            weights,
            dctx.reshape(seq, heads, head_dim),
            preferred_element_type=jnp.float32,
        )
        dvals = dvals.reshape(seq, inner).astype(jnp.bfloat16)
        dx = (
            dy.astype(jnp.float32) + jnp.dot(dvals, wv.T, preferred_element_type=jnp.float32)
        ).astype(jnp.bfloat16)
        return (context, dvals, dx)

    def skip_step(operands):
        return (
            jnp.zeros((seq, inner), jnp.bfloat16),
            jnp.zeros((seq, inner), jnp.bfloat16),
            jnp.zeros((seq, width), jnp.bfloat16),
        )

    ctx_store = jnp.zeros((micro, seq, inner), jnp.bfloat16)
    dv_store = jnp.zeros((micro, seq, inner), jnp.bfloat16)
    dy_store = jnp.zeros((micro, seq, width), jnp.bfloat16)
    dx_store = jnp.zeros((micro, seq, width), jnp.bfloat16)
    incoming = jnp.zeros((seq, width), jnp.bfloat16)
    last_turn = micro + npipe - 2
    for turn in range(micro + npipe - 1):
        step = turn - (npipe - 1 - section)
        valid = jnp.logical_and(step >= 0, step < micro)
        slot = jnp.clip(step, 0, micro - 1)
        batch = order[slot]
        dy = jnp.where(
            section == npipe - 1, lax.dynamic_index_in_dim(top_grad, slot, 0, False), incoming
        )
        xm = lax.dynamic_index_in_dim(inputs, batch, 0, False)
        pm = lax.dynamic_index_in_dim(probs, batch, 0, False)
        context, dvals, dx = lax.cond(valid, backward_step, skip_step, (xm, pm, dy))
        ctx_store = jnp.where(
            valid, lax.dynamic_update_index_in_dim(ctx_store, context, batch, 0), ctx_store
        )
        dv_store = jnp.where(
            valid, lax.dynamic_update_index_in_dim(dv_store, dvals, batch, 0), dv_store
        )
        dy_store = jnp.where(
            valid, lax.dynamic_update_index_in_dim(dy_store, dy, batch, 0), dy_store
        )
        dx_store = jnp.where(
            valid, lax.dynamic_update_index_in_dim(dx_store, dx, slot, 0), dx_store
        )
        if turn < last_turn:
            incoming = passed_along(dx, "pipe", -1)
    x_flat = inputs.reshape(micro * seq, width)
    dv_flat = dv_store.reshape(micro * seq, inner)
    dy_flat = dy_store.reshape(micro * seq, width)
    ctx_flat = ctx_store.reshape(micro * seq, inner)
    contract = (((0,), (0,)), ((), ()))
    ck_float = check_rows.astype(jnp.float32)
    rows = width // lax.axis_size("dp")
    columns = x_flat
    grad_v = lax.psum_scatter(
        (
            lax.dot_general(columns, dv_flat, contract, preferred_element_type=jnp.float32)
            * grad_scale
        ).astype(jnp.bfloat16),
        "dp",
        scatter_dimension=0,
        tiled=True,
    ).astype(jnp.float32)
    columns = dy_flat
    grad_o = lax.psum_scatter(
        (
            lax.dot_general(columns, ctx_flat, contract, preferred_element_type=jnp.float32)
            * grad_scale
        ).astype(jnp.bfloat16),
        "dp",
        scatter_dimension=0,
        tiled=True,
    ).astype(jnp.float32)
    first_row = lax.axis_index("dp") * rows
    ck_part = lax.dynamic_slice_in_dim(ck_float, first_row, rows, 1)
    local_checks = check_scale * jnp.stack(
        [
            jnp.dot(ck_part, grad_v, precision=lax.Precision.HIGHEST),
            jnp.dot(ck_part, grad_o, precision=lax.Precision.HIGHEST),
        ]
    )
    check_sum = lax.psum(local_checks, "dp")
    first_grads = from_root(dx_store, "pipe", 0)
    share = width // npipe
    own_part = lax.dynamic_slice_in_dim(first_grads, section * share, share, 2)
    return (grad_v[None], grad_o[None], check_sum[None], own_part)


def solution(mesh):
    return jax.shard_map(
        on_device,
        mesh=mesh,
        in_specs=(
            P("pipe", None, "dp", None),
            P("pipe", None, "dp", None, None, None),
            P("pipe", None, None),
            P("pipe", None, None),
            P(None, "dp", "pipe"),
            P(),
            P(),
        ),
        out_specs=(
            P("pipe", "dp", None),
            P("pipe", "dp", None),
            P("pipe", None, None, None),
            P(None, "dp", "pipe"),
        ),
        check_vma=False,
    )
```

profile of v0, /device:TPU:16, one launch (start us, length us, event | category | flops | bytes accessed | tf_op | source)
XLA Modules:
  0.0 1039.1 jit_solution(13033466347937102646)
XLA Ops:
  8.0 1.5 fusion.131
  11.5 44.0 %all-gather.2.cloned.1.call-done = bf16[2,160,6144]{2,1,0:T(8,128)(2,1)} async-done(((bf16[2,160,1536]{2,1,0:T(8,128)(2,1)}), bf16[2,160,6144]{2,1,0:T(8,128)(2,1)}) %all-gather.2.cloned.1.call-update) | async-done | bytes 3932176 | tf_op jit(solution)/shard_map/all_gather | solution.py:34
  55.5 2.5 broadcast.104.clone
  57.9 4.3 select_dynamic-update-slice_fusion.5
  62.5 1.8 conditional.5
  62.5 1.6 broadcast.92
  67.5 3.3 collective-permute-done
  70.8 5.2 fusion.125
  76.1 3.2 conditional.6
  76.1 1.5 broadcast.94
  77.6 1.5 broadcast_in_dim.112
  86.4 19.1 %collective-permute-done.1 = bf16[160,6144]{1,0:T(8,128)(2,1)S(1)} collective-permute-done((bf16[160,6144]{1,0:T(8,128)(2,1)}, bf16[160,6144]{1,0:T(8,128)(2,1)S(1)}, u32[]{:S(2)}, u32[]{:S(2)}) %collective-permute-start.1) | collective-permute-done | bytes 1966112 | tf_op jit(solution)/shard_map/ppermute | solution.py:10
  106.8 5.4 fusion.124
  112.9 4.6 conditional.7
  112.9 1.5 broadcast.95
  114.5 1.5 broadcast_in_dim.115
  117.6 1.4 collective-permute-start.2
  119.0 2.4 broadcast.104
  121.4 1.7 select_dynamic-update-slice_fusion.4
  123.1 3.9 select_dynamic-update-slice_fusion.3
  127.0 53.4 %collective-permute-done.2 = bf16[160,6144]{1,0:T(8,128)(2,1)S(1)} collective-permute-done((bf16[160,6144]{1,0:T(8,128)(2,1)}, bf16[160,6144]{1,0:T(8,128)(2,1)S(1)}, u32[]{:S(2)}, u32[]{:S(2)}) %collective-permute-start.2) | collective-permute-done | bytes 1966112 | tf_op jit(solution)/shard_map/ppermute | solution.py:10
  180.4 4.1 fusion.123
  184.6 21.8 %conditional.8 = (bf16[160,6144]{1,0:T(8,128)(2,1)}, bf16[1,160,768]{2,1,0:T(8,128)(2,1)}, bf16[1,160,768]{2,1,0:T(8,128)(2,1)S(1)}, bf16[1,160,6144]{2,1,0:T(8,128)(2,1)}) conditional(s32[]{:T(128)} %convert_element_type.329, () %tuple.104, (bf16[160,6144]{1,0:T(8,128)(2,1)S(1)}, bf16[768,6144]{1,0:T(8,128)(2,1)S(1)}, ...), branch_computations={%region_6.7_spmd, %region_7.8_spmd} | conditional | flops 4612700160 | bytes 89258160 | solution.py:83
  185.0 3.9 fusion.81
  189.7 1.5 convolution_convert_fusion.9
  191.3 8.3 fusion.73
  199.6 3.2 copy.226
  202.8 1.8 fusion.82
  207.7 3.5 select_dynamic-update-slice_fusion.2
  211.2 4.2 select_dynamic-update-slice_fusion.1
  215.4 17.1 %collective-permute-done.3 = bf16[160,6144]{1,0:T(8,128)(2,1)S(1)} collective-permute-done((bf16[160,6144]{1,0:T(8,128)(2,1)}, bf16[160,6144]{1,0:T(8,128)(2,1)S(1)}, u32[]{:S(2)}, u32[]{:S(2)}) %collective-permute-start.3) | collective-permute-done | bytes 1966112 | tf_op jit(solution)/shard_map/ppermute | solution.py:10
  232.6 4.0 fusion.122
  236.6 18.0 %conditional.9 = (bf16[1,160,768]{2,1,0:T(8,128)(2,1)}, bf16[1,160,768]{2,1,0:T(8,128)(2,1)}, bf16[1,160,6144]{2,1,0:T(8,128)(2,1)}) conditional(s32[]{:T(128)} %convert_element_type.330, () %tuple.106, (bf16[1,2,160,6144]{3,2,1,0:T(8,128)(2,1)}, s32[]{:T(128)}, bf16[6144,768]{1,0:T(8,128)(2,1)}, bf16[1,2,1,6,160,160]{5,4,3,2,1,0:T(8,128)(2,1)S(1)}, ...), branch_computations={%region_8.9_spmd, %region_9.10_spmd} | conditional | flops 4612700160 | bytes 98173048 | solution.py:83
  236.8 1.4 copy.102
  238.2 7.1 fusion.105
  245.6 4.6 fusion.97
  250.2 1.8 fusion.106
  254.6 4.1 select_dynamic-update-slice_fusion
  258.7 4.2 broadcast_select_fusion
  266.4 9.6 fusion.120
  278.1 9.6 fusion.121
  287.7 12.7 %copy.109 = bf16[6144,768]{1,0:T(8,128)(2,1)} copy(bf16[6144,768]{0,1:T(8,128)(2,1)} %fusion.121) | data formatting | bytes 18874368
  300.4 53.4 %all-reduce.2.cloned.1.call-done = bf16[2,160,6144]{2,1,0:T(8,128)(2,1)} async-done(((bf16[2,160,6144]{2,1,0:T(8,128)(2,1)}), bf16[2,160,6144]{2,1,0:T(8,128)(2,1)}) %all-reduce.2.cloned.1.call-update) | async-done | bytes 3932176 | tf_op jit(solution)/shard_map/psum | solution.py:15
  353.9 2.2 constant_dynamic-slice_fusion
  356.1 245.0 %reduce-scatter.5.cloned.1.call-done = bf16[192,768]{1,0:T(8,128)(2,1)} async-done(((bf16[6144,768]{1,0:T(8,128)(2,1)}), bf16[192,768]{1,0:T(8,128)(2,1)}) %reduce-scatter.5.cloned.1.call-update) | async-done | bytes 294928 | tf_op jit(solution)/shard_map/reduce_scatter | solution.py:116
  601.0 1.3 convolution_bitcast_fusion
  602.3 243.8 %reduce-scatter.7.cloned.1.call-done = bf16[192,768]{1,0:T(8,128)(2,1)} async-done(((bf16[6144,768]{1,0:T(8,128)(2,1)}), bf16[192,768]{1,0:T(8,128)(2,1)}) %reduce-scatter.7.cloned.1.call-update) | async-done | bytes 294928
  847.4 181.8 %psum.14 = f32[1,2,8,768]{3,2,1,0:T(8,128)} all-reduce(f32[1,2,8,768]{3,2,1,0:T(8,128)S(1)} %fusion.127), channel_id=1, replica_groups=mesh['pipe'=4,'dp'=32] {'dp'}, use_global_device_ids=true, to_apply=%region_12.13 | all-reduce | flops 12288 | bytes 98304 | tf_op jit(solution)/shard_map/psum | solution.py:133
  (107 shorter events, 24.1 us)
Async XLA Ops:
  7.2 48.3 %all-gather.2.cloned.1.call-start = ((), (), s32[]{:S(2)}) async-start(), calls=%async_computation.2 | async-start | bytes 4915200 | tf_op jit(solution)/shard_map/all_gather | solution.py:34
  7.9 346.0 %all-reduce.2.cloned.1.call-start = ((), (), s32[]{:S(2)}) async-start(), calls=%async_computation.4 | async-start | bytes 7864320 | tf_op jit(solution)/shard_map/psum | solution.py:15
  55.5 7.0 copy-start.1
  57.9 4.6 copy-start.5
  64.3 6.5 copy-start.6
  64.3 11.7 %copy-start.20 = (bf16[1,160,768]{2,1,0:T(8,128)(2,1)}, bf16[1,160,768]{2,1,0:T(8,128)(2,1)S(1)}, u32[]{:S(2)}) copy-start(bf16[1,160,768]{2,1,0:T(8,128)(2,1)S(1)} %get-tuple-element.362) | copy-start | bytes 737284
  64.4 11.7 %copy-start.22 = (bf16[1,160,768]{2,1,0:T(8,128)(2,1)}, bf16[1,160,768]{2,1,0:T(8,128)(2,1)S(1)}, u32[]{:S(2)}) copy-start(bf16[1,160,768]{2,1,0:T(8,128)(2,1)S(1)} %get-tuple-element.353) | copy-start | bytes 737284
  64.4 6.5 collective-permute-start
  79.3 33.6 %copy-start.17 = (bf16[1,160,768]{2,1,0:T(8,128)(2,1)}, bf16[1,160,768]{2,1,0:T(8,128)(2,1)S(1)}, u32[]{:S(2)}) copy-start(bf16[1,160,768]{2,1,0:T(8,128)(2,1)S(1)} %get-tuple-element.355) | copy-start | bytes 737284
  79.3 26.1 %collective-permute-start.1 = (bf16[160,6144]{1,0:T(8,128)(2,1)}, bf16[160,6144]{1,0:T(8,128)(2,1)S(1)}, u32[]{:S(2)}, u32[]{:S(2)}) collective-permute-start(bf16[160,6144]{1,0:T(8,128)(2,1)} %get-tuple-element.356), channel_id=1, source_target_pairs={{32,0},{64,32},{96,64},{33,1},{65,33},{97,65},{34,2},{66,34},{98,6... | collective-permute-start | bytes 5898248 | tf_op jit(solution)/shard_map/ppermute | solution.py:10
  105.5 1.3 copy-start.14
  106.8 6.1 copy-start.2
  117.6 3.8 copy-start.7
  117.6 62.9 %collective-permute-start.2 = (bf16[160,6144]{1,0:T(8,128)(2,1)}, bf16[160,6144]{1,0:T(8,128)(2,1)S(1)}, u32[]{:S(2)}, u32[]{:S(2)}) collective-permute-start(bf16[160,6144]{1,0:T(8,128)(2,1)} %get-tuple-element.358), channel_id=1, source_target_pairs={{32,0},{64,32},{96,64},{33,1},{65,33},{97,65},{34,2},{66,34},{98,6... | collective-permute-start | bytes 5898248 | tf_op jit(solution)/shard_map/ppermute | solution.py:10
  121.4 63.2 %slice-start.12 = ((s8[9437184]{0:T(1024)(128)(4,1)}), s8[4194304]{0:T(1024)(128)(4,1)S(1)}, s32[]{:S(2)}) async-start(s8[9437184]{0:T(1024)(128)(4,1)} %bitcast.268), calls=%async_computation.18 | async-start | bytes 8388608
  123.1 57.3 %copy-start.3 = (bf16[2,160,6144]{2,1,0:T(8,128)(2,1)S(1)}, bf16[2,160,6144]{2,1,0:T(8,128)(2,1)}, u32[]{:S(2)}) copy-start(bf16[2,160,6144]{2,1,0:T(8,128)(2,1)} %all-gather.2.cloned.1.call-done) | copy-start | bytes 11796484
  123.1 61.5 %slice-start.13 = ((s8[9437184]{0:T(1024)(128)(4,1)}), s8[4194304]{0:T(1024)(128)(4,1)S(1)}, s32[]{:S(2)}) async-start(s8[9437184]{0:T(1024)(128)(4,1)} %bitcast.268), calls=%async_computation.19 | async-start | bytes 8388608
  180.4 4.1 slice-start.14
  189.7 13.1 %slice-start.9 = ((s8[9437184]{0:T(1024)(128)(4,1)}), s8[4194304]{0:T(1024)(128)(4,1)S(1)}, s32[]{:S(2)}) async-start(s8[9437184]{0:T(1024)(128)(4,1)} %bitcast.262), calls=%async_computation.15 | async-start | bytes 8388608 | tf_op jit(solution)/shard_map/cond
  191.2 11.5 %slice-start.10 = ((s8[9437184]{0:T(1024)(128)(4,1)}), s8[4194304]{0:T(1024)(128)(4,1)S(1)}, s32[]{:S(2)}) async-start(s8[9437184]{0:T(1024)(128)(4,1)} %bitcast.262), calls=%async_computation.16 | async-start | bytes 8388608 | tf_op jit(solution)/shard_map/cond
  191.3 11.5 %slice-start.11 = ((s8[9437184]{0:T(1024)(128)(4,1)}), s8[1048576]{0:T(1024)(128)(4,1)S(1)}, s32[]{:S(2)}) async-start(s8[9437184]{0:T(1024)(128)(4,1)} %bitcast.262), calls=%async_computation.17 | async-start | bytes 2097152 | tf_op jit(solution)/shard_map/cond
  199.6 3.2 copy-start.11
  202.8 1.8 copy-start.28
  206.4 9.0 copy-start.24
  206.4 26.1 %collective-permute-start.3 = (bf16[160,6144]{1,0:T(8,128)(2,1)}, bf16[160,6144]{1,0:T(8,128)(2,1)S(1)}, u32[]{:S(2)}, u32[]{:S(2)}) collective-permute-start(bf16[160,6144]{1,0:T(8,128)(2,1)} %get-tuple-element.360), channel_id=1, source_target_pairs={{32,0},{64,32},{96,64},{33,1},{65,33},{97,65},{34,2},{66,34},{98,6... | collective-permute-start | bytes 5898248 | tf_op jit(solution)/shard_map/ppermute | solution.py:10
  211.2 21.4 %copy-start.4 = (bf16[2,160,6144]{2,1,0:T(8,128)(2,1)S(1)}, bf16[2,160,6144]{2,1,0:T(8,128)(2,1)}, u32[]{:S(2)}) copy-start(bf16[2,160,6144]{2,1,0:T(8,128)(2,1)} %all-gather.2.cloned.1.call-done) | copy-start | bytes 11796484
  238.2 7.1 copy-start.13
  238.2 7.4 copy-start
  245.6 4.6 copy-start.12
  262.9 0.9 copy-start.23
  262.9 1.1 copy-start.21
  262.9 1.2 copy-start.18
  263.0 338.1 %reduce-scatter.5.cloned.1.call-start = ((), (), s32[]{:S(2)}) async-start(), calls=%async_computation.3 | async-start | bytes 9732096 | tf_op jit(solution)/shard_map/reduce_scatter | solution.py:116
  276.0 1.0 copy-start.25
  276.1 570.1 %reduce-scatter.7.cloned.1.call-start = ((), (), s32[]{:S(2)}) async-start(), calls=%async_computation.5 | async-start | bytes 9732096
  601.0 430.5 %copy-start.16 = (bf16[192,768]{1,0:T(8,128)(2,1)S(1)}, bf16[192,768]{1,0:T(8,128)(2,1)}, u32[]{:S(2)}) copy-start(bf16[192,768]{1,0:T(8,128)(2,1)} %reduce-scatter.5.cloned.1.call-done) | copy-start | bytes 884740
Sparse Core Ops, SparseCore 0:
  9.7 45.7 all-gather.1
  263.1 90.7 all-reduce.1
  359.2 241.7 reduce-scatter.4
  606.2 239.8 reduce-scatter.6
where the time goes:
time: 1050 us; the launch traced here: 1040 us
  waiting for transfers between devices  680 us (65%)
  blocking collectives  182 us (17%)
  matrix products  51.8 us (5%)
  other arithmetic  49.2 us (5%)
  local copies, waits for them, and re-layouts  45.9 us (4%)
  between operations  23.8 us (2%)
    reduce_scatter x1, waiting for transfers between devices, on_device(): lax.psum_scatter((lax.dot_general(columns, ctx_flat, contract, preferred_...  245 us
    unnamed x5, waiting for transfers between devices  245 us
    psum x1, blocking collectives, on_device(): check_sum = lax.psum(local_checks, 'dp')  182 us
    ppermute x4, waiting for transfers between devices, passed_along(): return lax.ppermute(block, axis, route)  93 us
    psum x1, waiting for transfers between devices, from_root(): return lax.psum(jnp.where(mine, array, jnp.zeros_like(array)), axis)  53.4 us
    all_gather x1, waiting for transfers between devices, on_device(): top_grad = lax.all_gather(out_grad, 'pipe', axis=2, tiled=True)  44 us
    select_n x5, other arithmetic, on_device(): jnp.where(valid, lax.dynamic_update_index_in_dim(dy_store, dy, batch, 0),...  23 us
  transfers between devices with their start and end apart: 8, of which 8 were waited for; matrix products, arithmetic and copies ran while one was open for 5% of the time, Pallas kernels for 0%

commit v1 on v0

--- a/solution.py
+++ b/solution.py
@@ -31,7 +31,9 @@
     grad_scale = jnp.float32((micro * seq * lax.axis_size("dp")) ** (-0.5))
     check_scale = jnp.float32(width ** (-0.5))
     causal = (jnp.arange(seq)[:, None] >= jnp.arange(seq)[None, :]).astype(jnp.bfloat16)
-    top_grad = lax.all_gather(out_grad, "pipe", axis=2, tiled=True)
+    top_grad = jnp.concatenate(
+        lax.all_to_all(jnp.stack([out_grad] * lax.axis_size("pipe")), "pipe", 0, 0), axis=2
+    )
 
     def backward_step(operands):
         xm, pm, dy = operands

time: 1050 us -> 1000 us (0.952)
  waiting for transfers between devices: 680 us -> 626 us
  local copies, waits for them, and re-layouts: 45.9 us -> 60 us
    reduce_scatter x1, waiting for transfers between devices: 245 us -> 186 us  [on_device(): lax.psum_scatter((lax.dot_general(columns, ctx_flat, contract, preferred_...]
    all_gather x1 -> x0, waiting for transfers between devices: 44 us -> none  [on_device(): top_grad = lax.all_gather(out_grad, 'pipe', axis=2, tiled=True)]
    all_to_all x0 -> x1, waiting for transfers between devices: none -> 42.7 us  [on_device(): lax.all_to_all(jnp.stack([out_grad] * lax.axis_size('pipe')), 'pipe', 0, 0)]
    unnamed x43 -> x61, local copies, waits for them, and re-layouts: 18.5 us -> 28 us
    unnamed x5 -> x4, waiting for transfers between devices: 245 us -> 244 us
where the time goes in v1:
time: 1000 us; the launch traced here: 995 us
  waiting for transfers between devices  626 us (63%)
  blocking collectives  182 us (18%)
  local copies, waits for them, and re-layouts  60 us (6%)
  matrix products  50.2 us (5%)
  other arithmetic  40.1 us (4%)
  between operations  26 us (3%)
  starting transfers between devices  10.5 us (1%)
    unnamed x4, waiting for transfers between devices  244 us
    reduce_scatter x1, waiting for transfers between devices, on_device(): lax.psum_scatter((lax.dot_general(columns, ctx_flat, contract, preferred_...  186 us
    psum x1, blocking collectives, on_device(): check_sum = lax.psum(local_checks, 'dp')  182 us
    ppermute x4, waiting for transfers between devices, passed_along(): return lax.ppermute(block, axis, route)  91.2 us
    psum x1, waiting for transfers between devices, from_root(): return lax.psum(jnp.where(mine, array, jnp.zeros_like(array)), axis)  62 us
    all_to_all x1, waiting for transfers between devices, on_device(): lax.all_to_all(jnp.stack([out_grad] * lax.axis_size('pipe')), 'pipe', 0, 0)  42.7 us
    unnamed x61, local copies, waits for them, and re-layouts  28 us
  transfers between devices with their start and end apart: 8, of which 8 were waited for; matrix products, arithmetic and copies ran while one was open for 5% of the time, Pallas kernels for 0%

profile of v1, /device:TPU:16, one launch (start us, length us, event | category | flops | bytes accessed | tf_op | source)
XLA Modules:
  0.0 995.1 jit_solution(7627025668109115449)
XLA Ops:
  8.0 3.5 stack.16
  11.5 4.9 all-to-all-start
  19.1 42.7 %all-to-all-done = bf16[4,2,160,1536]{3,2,1,0:T(8,128)(2,1)} async-done(((bf16[4,2,160,1536]{3,2,1,0:T(8,128)(2,1)}), bf16[4,2,160,1536]{3,2,1,0:T(8,128)(2,1)}, u32[]{:S(2)}, u32[]{:S(2)}) %all-to-all-start) | async-done | bytes 3932192 | tf_op jit(solution)/shard_map/all_to_all | solution.py:35
  61.8 2.8 copy.163
  66.9 2.9 slice-done.14
  69.9 3.0 conditional.5
  69.9 1.5 broadcast.94
  71.4 1.5 broadcast_in_dim.109
  77.5 2.9 collective-permute-done
  81.6 5.3 fusion.125
  86.9 3.2 conditional.6
  86.9 1.5 broadcast.96
  88.4 1.5 broadcast_in_dim.112
  97.3 18.2 %collective-permute-done.1 = bf16[160,6144]{1,0:T(8,128)(2,1)S(1)} collective-permute-done((bf16[160,6144]{1,0:T(8,128)(2,1)}, bf16[160,6144]{1,0:T(8,128)(2,1)S(1)}, u32[]{:S(2)}, u32[]{:S(2)}) %collective-permute-start.1) | collective-permute-done | bytes 1966112 | tf_op jit(solution)/shard_map/ppermute | solution.py:10
  116.7 5.4 fusion.124
  122.8 4.8 conditional.7
  122.8 1.5 broadcast.97
  124.3 1.5 broadcast_in_dim.115
  129.0 2.5 broadcast.106
  131.4 1.6 select_dynamic-update-slice_fusion.4
  133.1 4.1 select_dynamic-update-slice_fusion.3
  137.1 53.1 %collective-permute-done.2 = bf16[160,6144]{1,0:T(8,128)(2,1)S(1)} collective-permute-done((bf16[160,6144]{1,0:T(8,128)(2,1)}, bf16[160,6144]{1,0:T(8,128)(2,1)S(1)}, u32[]{:S(2)}, u32[]{:S(2)}) %collective-permute-start.2) | collective-permute-done | bytes 1966112 | tf_op jit(solution)/shard_map/ppermute | solution.py:10
  191.4 1.9 copy-done.7
  193.3 21.5 %conditional.8 = (bf16[160,6144]{1,0:T(8,128)(2,1)}, bf16[1,160,768]{2,1,0:T(8,128)(2,1)}, bf16[1,160,768]{2,1,0:T(8,128)(2,1)S(1)}, bf16[1,160,6144]{2,1,0:T(8,128)(2,1)}) conditional(s32[]{:T(128)} %convert_element_type.329, () %tuple.104, (bf16[160,6144]{1,0:T(8,128)(2,1)S(1)}, bf16[768,6144]{1,0:T(8,128)(2,1)S(1)}, ...), branch_computations={%region_6.7_spmd, %region_7.8_spmd} | conditional | flops 4612700160 | bytes 89258160 | solution.py:85
  193.5 3.9 fusion.81
  198.2 1.5 convolution_convert_fusion.9
  199.7 8.3 fusion.73
  208.0 3.2 copy.264
  211.2 1.8 fusion.82
  216.2 3.6 select_dynamic-update-slice_fusion.2
  219.8 4.2 select_dynamic-update-slice_fusion.1
  223.9 17.1 %collective-permute-done.3 = bf16[160,6144]{1,0:T(8,128)(2,1)S(1)} collective-permute-done((bf16[160,6144]{1,0:T(8,128)(2,1)}, bf16[160,6144]{1,0:T(8,128)(2,1)S(1)}, u32[]{:S(2)}, u32[]{:S(2)}) %collective-permute-start.3) | collective-permute-done | bytes 1966112 | tf_op jit(solution)/shard_map/ppermute | solution.py:10
  242.3 1.9 copy-done.9
  244.2 18.1 %conditional.9 = (bf16[1,160,768]{2,1,0:T(8,128)(2,1)}, bf16[1,160,768]{2,1,0:T(8,128)(2,1)}, bf16[1,160,6144]{2,1,0:T(8,128)(2,1)}) conditional(s32[]{:T(128)} %convert_element_type.330, () %tuple.106, (bf16[1,2,160,6144]{3,2,1,0:T(8,128)(2,1)}, s32[]{:T(128)}, bf16[6144,768]{1,0:T(8,128)(2,1)}, bf16[1,2,1,6,160,160]{5,4,3,2,1,0:T(8,128)(2,1)S(1)}, ...), branch_computations={%region_8.9_spmd, %region_9.10_spmd} | conditional | flops 4612700160 | bytes 98173048 | solution.py:85
  244.4 1.4 copy.139
  245.8 7.1 fusion.105
  253.2 4.6 fusion.97
  257.9 1.8 fusion.106
  262.3 4.1 select_dynamic-update-slice_fusion
  266.4 4.2 broadcast_select_fusion
  274.2 7.6 fusion.120
  283.8 10.0 %fusion.121 = bf16[6144,768]{0,1:T(8,128)(2,1)} fusion(bf16[320,768]{1,0:T(8,128)(2,1)S(1)} %bitcast.281, bf16[320,6144]{1,0:T(8,128)(2,1)} %bitcast.282), kind=kOutput, calls=%fused_computation.128 | convolution fusion | flops 3029336064 | bytes 13860864 | tf_op jit(solution)/shard_map/dot_general | solution.py:110
  293.8 12.1 %copy.146 = bf16[6144,768]{1,0:T(8,128)(2,1)} copy(bf16[6144,768]{0,1:T(8,128)(2,1)} %fusion.121) | data formatting | bytes 18874368
  306.0 62.0 %all-reduce.2.cloned.1.call-done = bf16[2,160,6144]{2,1,0:T(8,128)(2,1)} async-done(((bf16[2,160,6144]{2,1,0:T(8,128)(2,1)}), bf16[2,160,6144]{2,1,0:T(8,128)(2,1)}) %all-reduce.2.cloned.1.call-update) | async-done | bytes 3932176 | tf_op jit(solution)/shard_map/psum | solution.py:15
  367.9 2.3 constant_dynamic-slice_fusion
  370.2 185.7 %reduce-scatter.5.cloned.1.call-done = bf16[192,768]{1,0:T(8,128)(2,1)} async-done(((bf16[6144,768]{1,0:T(8,128)(2,1)}), bf16[192,768]{1,0:T(8,128)(2,1)}) %reduce-scatter.5.cloned.1.call-update) | async-done | bytes 294928 | tf_op jit(solution)/shard_map/reduce_scatter | solution.py:118
  557.1 244.2 %reduce-scatter.7.cloned.1.call-done = bf16[192,768]{1,0:T(8,128)(2,1)} async-done(((bf16[6144,768]{1,0:T(8,128)(2,1)}), bf16[192,768]{1,0:T(8,128)(2,1)}) %reduce-scatter.7.cloned.1.call-update) | async-done | bytes 294928
  802.6 181.5 %psum.14 = f32[1,2,8,768]{3,2,1,0:T(8,128)} all-reduce(f32[1,2,8,768]{3,2,1,0:T(8,128)S(1)} %fusion.127), channel_id=1, replica_groups=mesh['pipe'=4,'dp'=32] {'dp'}, use_global_device_ids=true, to_apply=%region_12.13 | all-reduce | flops 12288 | bytes 98304 | tf_op jit(solution)/shard_map/psum | solution.py:135
  (127 shorter events, 33.6 us)
Async XLA Ops:
  11.5 5.0 copy-start.34
  11.5 55.4 %slice-start.12 = ((s8[9437184]{0:T(1024)(128)(4,1)}), s8[1048576]{0:T(1024)(128)(4,1)S(1)}, s32[]{:S(2)}) async-start(s8[9437184]{0:T(1024)(128)(4,1)} %bitcast.269), calls=%async_computation.18 | async-start | bytes 2097152
  11.5 50.3 %all-to-all-start = ((bf16[4,2,160,1536]{3,2,1,0:T(8,128)(2,1)}), bf16[4,2,160,1536]{3,2,1,0:T(8,128)(2,1)}, u32[]{:S(2)}, u32[]{:S(2)}) async-start(bf16[4,2,160,1536]{3,2,1,0:T(8,128)(2,1)} %stack.16), calls=%async_computation | async-start | bytes 7864320 | tf_op jit(solution)/shard_map/all_to_all | solution.py:35
  16.4 351.5 %all-reduce.2.cloned.1.call-start = ((), (), s32[]{:S(2)}) async-start(), calls=%async_computation.4 | async-start | bytes 7864320 | tf_op jit(solution)/shard_map/psum | solution.py:15
  61.8 5.1 slice-start.13
  64.6 2.0 copy-start.2
  64.6 5.2 slice-start.14
  65.1 4.8 copy-start.11
  66.6 3.3 copy-start.5
  72.9 0.7 copy-start.25
  73.6 0.7 copy-start.27
  74.3 6.1 collective-permute-start
  80.4 1.3 copy-start.19
  90.1 32.7 %copy-start.22 = (bf16[1,160,768]{2,1,0:T(8,128)(2,1)}, bf16[1,160,768]{2,1,0:T(8,128)(2,1)S(1)}, u32[]{:S(2)}) copy-start(bf16[1,160,768]{2,1,0:T(8,128)(2,1)S(1)} %get-tuple-element.355) | copy-start | bytes 737284
  90.1 25.3 %collective-permute-start.1 = (bf16[160,6144]{1,0:T(8,128)(2,1)}, bf16[160,6144]{1,0:T(8,128)(2,1)S(1)}, u32[]{:S(2)}, u32[]{:S(2)}) collective-permute-start(bf16[160,6144]{1,0:T(8,128)(2,1)} %get-tuple-element.356), channel_id=1, source_target_pairs={{32,0},{64,32},{96,64},{33,1},{65,33},{97,65},{34,2},{66,34},{98,6... | collective-permute-start | bytes 5898248 | tf_op jit(solution)/shard_map/ppermute | solution.py:10
  115.4 1.3 copy-start.18
  116.7 6.1 copy-start.1
  127.7 62.5 %collective-permute-start.2 = (bf16[160,6144]{1,0:T(8,128)(2,1)}, bf16[160,6144]{1,0:T(8,128)(2,1)S(1)}, u32[]{:S(2)}, u32[]{:S(2)}) collective-permute-start(bf16[160,6144]{1,0:T(8,128)(2,1)} %get-tuple-element.358), channel_id=1, source_target_pairs={{32,0},{64,32},{96,64},{33,1},{65,33},{97,65},{34,2},{66,34},{98,6... | collective-permute-start | bytes 5898248 | tf_op jit(solution)/shard_map/ppermute | solution.py:10
  129.0 61.2 %copy-start.6 = (bf16[2,160,6144]{2,1,0:T(8,128)(2,1)S(1)}, bf16[2,160,6144]{2,1,0:T(8,128)(2,1)}, u32[]{:S(2)}) copy-start(bf16[2,160,6144]{2,1,0:T(8,128)(2,1)} %get-tuple-element.536) | copy-start | bytes 11796484
  131.4 60.0 %slice-start.15 = ((s8[9437184]{0:T(1024)(128)(4,1)}), s8[4194304]{0:T(1024)(128)(4,1)S(1)}, s32[]{:S(2)}) async-start(s8[9437184]{0:T(1024)(128)(4,1)} %bitcast.273), calls=%async_computation.21 | async-start | bytes 8388608
  133.1 57.1 %copy-start.3 = (bf16[4,2,20,8,1536]{4,3,0,2,1:T(8,128)(2,1)S(1)}, bf16[4,2,20,8,1536]{4,3,0,2,1:T(8,128)(2,1)}, u32[]{:S(2)}) copy-start(bf16[4,2,20,8,1536]{4,3,0,2,1:T(8,128)(2,1)} %copy-done.2) | copy-start | bytes 11796484
  133.1 58.4 %slice-start.16 = ((s8[9437184]{0:T(1024)(128)(4,1)}), s8[4194304]{0:T(1024)(128)(4,1)S(1)}, s32[]{:S(2)}) async-start(s8[9437184]{0:T(1024)(128)(4,1)} %bitcast.273), calls=%async_computation.22 | async-start | bytes 8388608
  190.2 1.2 slice-start.17
  191.4 1.9 copy-start.7
  198.2 13.1 %slice-start.9 = ((s8[9437184]{0:T(1024)(128)(4,1)}), s8[4194304]{0:T(1024)(128)(4,1)S(1)}, s32[]{:S(2)}) async-start(s8[9437184]{0:T(1024)(128)(4,1)} %bitcast.265), calls=%async_computation.15 | async-start | bytes 8388608 | tf_op jit(solution)/shard_map/cond
  199.7 11.5 %slice-start.10 = ((s8[9437184]{0:T(1024)(128)(4,1)}), s8[4194304]{0:T(1024)(128)(4,1)S(1)}, s32[]{:S(2)}) async-start(s8[9437184]{0:T(1024)(128)(4,1)} %bitcast.265), calls=%async_computation.16 | async-start | bytes 8388608 | tf_op jit(solution)/shard_map/cond
  199.7 11.5 %slice-start.11 = ((s8[9437184]{0:T(1024)(128)(4,1)}), s8[1048576]{0:T(1024)(128)(4,1)S(1)}, s32[]{:S(2)}) async-start(s8[9437184]{0:T(1024)(128)(4,1)} %bitcast.265), calls=%async_computation.17 | async-start | bytes 2097152 | tf_op jit(solution)/shard_map/cond
  208.0 3.2 copy-start.15
  211.2 1.8 copy-start.33
  214.9 9.1 copy-start.29
  214.9 26.2 %collective-permute-start.3 = (bf16[160,6144]{1,0:T(8,128)(2,1)}, bf16[160,6144]{1,0:T(8,128)(2,1)S(1)}, u32[]{:S(2)}, u32[]{:S(2)}) collective-permute-start(bf16[160,6144]{1,0:T(8,128)(2,1)} %get-tuple-element.360), channel_id=1, source_target_pairs={{32,0},{64,32},{96,64},{33,1},{65,33},{97,65},{34,2},{66,34},{98,6... | collective-permute-start | bytes 5898248 | tf_op jit(solution)/shard_map/ppermute | solution.py:10
  216.2 24.9 %copy-start.8 = (bf16[2,160,6144]{2,1,0:T(8,128)(2,1)S(1)}, bf16[2,160,6144]{2,1,0:T(8,128)(2,1)}, u32[]{:S(2)}) copy-start(bf16[2,160,6144]{2,1,0:T(8,128)(2,1)} %copy-done.7) | copy-start | bytes 11796484
  219.8 21.3 %copy-start.4 = (bf16[4,2,20,8,1536]{4,3,0,2,1:T(8,128)(2,1)S(1)}, bf16[4,2,20,8,1536]{4,3,0,2,1:T(8,128)(2,1)}, u32[]{:S(2)}) copy-start(bf16[4,2,20,8,1536]{4,3,0,2,1:T(8,128)(2,1)} %copy-done.2) | copy-start | bytes 11796484
  242.3 1.9 copy-start.9
  245.8 7.1 copy-start.17
  245.8 7.4 copy-start
  253.2 4.7 copy-start.16
  270.6 0.9 copy-start.28
  270.6 1.1 copy-start.26
  270.6 1.2 copy-start.23
  270.6 285.2 %reduce-scatter.5.cloned.1.call-start = ((), (), s32[]{:S(2)}) async-start(), calls=%async_computation.3 | async-start | bytes 9732096 | tf_op jit(solution)/shard_map/reduce_scatter | solution.py:118
  270.7 3.5 copy-start.10
  281.8 0.9 copy-start.30
  281.8 519.5 %reduce-scatter.7.cloned.1.call-start = ((), (), s32[]{:S(2)}) async-start(), calls=%async_computation.5 | async-start | bytes 9732096
  555.8 430.5 %copy-start.21 = (bf16[192,768]{1,0:T(8,128)(2,1)S(1)}, bf16[192,768]{1,0:T(8,128)(2,1)}, u32[]{:S(2)}) copy-start(bf16[192,768]{1,0:T(8,128)(2,1)} %reduce-scatter.5.cloned.1.call-done) | copy-start | bytes 884740
Sparse Core Ops, SparseCore 0:
  270.7 97.1 all-reduce.1
Sparse Core Ops, SparseCore 1:
  281.9 273.9 reduce-scatter.4
  561.1 240.2 reduce-scatter.6
